TPU v7x, 256 devices: a whole 4x4x8 slice. The times are simulated.
256 devices in a mesh: blk: 32 (over z, x_lo, core), hd: 8 (over x_hi, y).
Axes of the slice: x: 4 (x_hi: 2, x_lo: 2; x = x_hi * 2 + x_lo), y: 4, z: 8, core: 2. Of those that a mesh axis runs over, the one named last changes fastest.
Arguments:
- queries: bfloat16 [16384, 4096], P(('blk', 'hd')), may hold values from -8 to 8
- keys: bfloat16 [16384, 1024], P(('blk', 'hd')), may hold values from -8 to 8
- values: bfloat16 [16384, 1024], P(('blk', 'hd')), may hold values from -6 to 6
Outputs:
- attended: bfloat16 [16384, 4096], P(('blk', 'hd'))
All inputs are finite; a program needn't handle non-finite values.
Results may differ from a plain program's by a relative error of at most 0.0044.
Values may be sent and summed in bfloat16 or wider, within the bound.
No kernel may reach another device: no remote copies, remote signals or barrier semaphores. Data moves between devices by JAX's collectives and lax.ppermute only.
A program may use at most 64 MiB of HBM per device.

v0:
```python
import jax
import jax.numpy as jnp
from jax import lax
from jax.sharding import PartitionSpec as P

H = 32
KV = 8
HD = 128
BLK = 256


def broadcast(array, axis, root):
    mine = lax.axis_index(axis) == root
    return lax.psum(jnp.where(mine, array, jnp.zeros_like(array)), axis)


def head_attention(query_part, key_part, value_part, visible, scaling):
    scores = (
        jnp.einsum("qd,kd->qk", query_part, key_part, preferred_element_type=jnp.float32) * scaling
    )
    masked = jnp.where(visible, scores, -jnp.inf)
    largest = jnp.max(masked, axis=1, keepdims=True)
    raised = jnp.exp(masked - largest)
    totals = jnp.sum(raised, axis=1, keepdims=True)
    weights = raised.astype(jnp.bfloat16)
    mixture = jnp.dot(weights, value_part, preferred_element_type=jnp.float32)
    return (mixture / totals).astype(jnp.bfloat16)


def shards(queries, keys, values):
    scaling = HD ** (-0.5)
    query_heads, key_heads, value_heads = (
        lax.all_to_all(queries, "hd", split_axis=1, concat_axis=0, tiled=True),
        lax.all_to_all(keys, "hd", split_axis=1, concat_axis=0, tiled=True),
        lax.all_to_all(values, "hd", split_axis=1, concat_axis=0, tiled=True),
    )
    anchor_keys, anchor_values = (
        broadcast(key_heads[:BLK], "blk", 0),
        broadcast(value_heads[:BLK], "blk", 0),
    )
    heads_here = query_heads.shape[1] // HD
    group_size = H // KV
    group_index = lax.axis_index("blk")
    positions = jnp.arange(BLK)[:, None]
    columns = jnp.arange(2 * BLK)[None, :]
    pieces = []
    for block_slot in range(2):
        anchored = 2 * group_index + block_slot > 0
        visible = jnp.where(columns < BLK, anchored, columns - BLK <= positions)
        start = block_slot * BLK
        head_outputs = []
        for head_slot in range(heads_here):
            kv_slot = head_slot // group_size
            query_part = query_heads[start : start + BLK, head_slot * HD : (head_slot + 1) * HD]
            key_part = jnp.concatenate(
                [anchor_keys, key_heads[start : start + BLK, kv_slot * HD : (kv_slot + 1) * HD]],
                axis=0,
            )
            value_part = jnp.concatenate(
                [
                    anchor_values,
                    value_heads[start : start + BLK, kv_slot * HD : (kv_slot + 1) * HD],
                ],
                axis=0,
            )
            head_outputs.append(head_attention(query_part, key_part, value_part, visible, scaling))
        pieces.append(jnp.concatenate(head_outputs, axis=1))
    attended = jnp.concatenate(pieces, axis=0)
    return lax.all_to_all(attended, "hd", split_axis=0, concat_axis=1, tiled=True)


def solution(mesh):
    placed = (P(("blk", "hd"), None), P(("blk", "hd"), None), P(("blk", "hd"), None))
    return jax.shard_map(
        shards, mesh=mesh, in_specs=placed, out_specs=P(("blk", "hd"), None), check_vma=False
    )
```

profile of v0, /device:TPU:98, one launch (start us, length us, event | category | flops | bytes accessed | tf_op | source)
XLA Modules:
  0.0 278.1 jit_solution(4570407309087471163)
XLA Ops:
  6.5 0.9 copy-done
  7.4 0.7 copy_bitcast_fusion.2
  8.1 6.0 %all-to-all-start = ((bf16[64,8,128]{2,0,1:T(8,128)(2,1)}), bf16[64,8,128]{2,0,1:T(8,128)(2,1)S(1)}, u32[]{:S(2)}, u32[]{:S(2)}) async-start(bf16[64,8,128]{2,0,1:T(8,128)(2,1)} %copy_bitcast_fusion.2), calls=%async_computation | async-start | bytes 262144 | tf_op jit(solution)/shard_map/all_to_all | solution.py:34
  14.2 1.6 copy_bitcast_fusion.1
  15.7 0.8 copy.25
  16.6 5.7 %all-to-all-done = bf16[64,8,128]{2,0,1:T(8,128)(2,1)S(1)} async-done(((bf16[64,8,128]{2,0,1:T(8,128)(2,1)}), bf16[64,8,128]{2,0,1:T(8,128)(2,1)S(1)}, u32[]{:S(2)}, u32[]{:S(2)}) %all-to-all-start) | async-done | bytes 131104 | tf_op jit(solution)/shard_map/all_to_all | solution.py:34
  22.2 3.4 %all-to-all-start.2 = ((bf16[64,8,128]{2,0,1:T(8,128)(2,1)}), bf16[64,8,128]{2,0,1:T(8,128)(2,1)S(1)}, u32[]{:S(2)}, u32[]{:S(2)}) async-start(bf16[64,8,128]{2,0,1:T(8,128)(2,1)} %copy_bitcast_fusion.1), calls=%async_computation.2 | async-start | bytes 262144 | tf_op jit(solution)/shard_map/all_to_all | solution.py:35
  25.6 8.0 %all-to-all-done.2 = bf16[64,8,128]{2,0,1:T(8,128)(2,1)S(1)} async-done(((bf16[64,8,128]{2,0,1:T(8,128)(2,1)}), bf16[64,8,128]{2,0,1:T(8,128)(2,1)S(1)}, u32[]{:S(2)}, u32[]{:S(2)}) %all-to-all-start.2) | async-done | bytes 131104 | tf_op jit(solution)/shard_map/all_to_all | solution.py:35
  33.6 3.5 %all-to-all-start.1 = ((bf16[64,8,512]{2,0,1:T(8,128)(2,1)}), bf16[64,8,512]{2,0,1:T(8,128)(2,1)S(1)}, u32[]{:S(2)}, u32[]{:S(2)}) async-start(bf16[64,8,512]{2,0,1:T(8,128)(2,1)} %bitcast.60), calls=%async_computation.1 | async-start | bytes 1048576 | tf_op jit(solution)/shard_map/all_to_all | solution.py:33
  37.2 0.7 broadcast_select_fusion
  37.9 207.2 %all-reduce.3.cloned.1.call-done = (bf16[256,128]{1,0:T(8,128)(2,1)}, bf16[256,128]{1,0:T(8,128)(2,1)}) async-done(((bf16[256,128]{1,0:T(8,128)(2,1)}, bf16[256,128]{1,0:T(8,128)(2,1)}), (bf16[256,128]{1,0:T(8,128)(2,1)}, bf16[256,128]{1,0:T(8,128)(2,1)})) %all-reduce.3.cloned.1.call-update) | async-done | bytes 131088 | tf_op jit(solution)/shard_map/psum | solution.py:14
  245.1 1.2 fusion.75
  246.3 0.3 fusion.74
  246.6 0.3 fusion.73
  246.9 0.3 fusion.72
  247.2 0.3 fusion.71
  247.5 0.3 fusion.70
  247.7 0.3 fusion.69
  248.0 0.3 fusion.68
  248.6 0.7 copy-done.2
  249.6 0.2 fusion.17
  249.9 0.2 fusion.18
  252.4 18.1 %all_to_all.70 = bf16[8,64,512]{2,1,0:T(8,128)(2,1)S(1)} all-to-all(bf16[8,64,512]{2,1,0:T(8,128)(2,1)S(1)} %bitcast.61), channel_id=1, replica_groups=mesh['blk'=32,'hd'=8] {'hd'}, dimensions={0} | all-to-all | bytes 1048576 | tf_op jit(solution)/shard_map/all_to_all | solution.py:69
  270.4 0.8 copy.21
  (29 shorter events, 2.8 us)
Async XLA Ops:
  6.5 0.9 copy-start
  7.4 8.3 %copy-start.1 = (bf16[64,4096]{1,0:T(8,128)(2,1)S(1)}, bf16[64,4096]{1,0:T(8,128)(2,1)}, u32[]{:S(2)}) copy-start(bf16[64,4096]{1,0:T(8,128)(2,1)} %param.3) | copy-start | bytes 1572868
  8.1 14.1 %all-to-all-start = ((bf16[64,8,128]{2,0,1:T(8,128)(2,1)}), bf16[64,8,128]{2,0,1:T(8,128)(2,1)S(1)}, u32[]{:S(2)}, u32[]{:S(2)}) async-start(bf16[64,8,128]{2,0,1:T(8,128)(2,1)} %copy_bitcast_fusion.2), calls=%async_computation | async-start | bytes 262144 | tf_op jit(solution)/shard_map/all_to_all | solution.py:34
  22.2 11.4 %all-to-all-start.2 = ((bf16[64,8,128]{2,0,1:T(8,128)(2,1)}), bf16[64,8,128]{2,0,1:T(8,128)(2,1)S(1)}, u32[]{:S(2)}, u32[]{:S(2)}) async-start(bf16[64,8,128]{2,0,1:T(8,128)(2,1)} %copy_bitcast_fusion.1), calls=%async_computation.2 | async-start | bytes 262144 | tf_op jit(solution)/shard_map/all_to_all | solution.py:35
  33.6 211.5 %all-to-all-start.1 = ((bf16[64,8,512]{2,0,1:T(8,128)(2,1)}), bf16[64,8,512]{2,0,1:T(8,128)(2,1)S(1)}, u32[]{:S(2)}, u32[]{:S(2)}) async-start(bf16[64,8,512]{2,0,1:T(8,128)(2,1)} %bitcast.60), calls=%async_computation.1 | async-start | bytes 1048576 | tf_op jit(solution)/shard_map/all_to_all | solution.py:33
  37.1 208.0 %all-reduce.3.cloned.1.call-start = ((), (), s32[]{:S(2)}) async-start(), calls=%async_computation.4 | async-start | bytes 262144 | tf_op jit(solution)/shard_map/psum | solution.py:14
  245.1 1.2 copy-start.3
  248.5 0.8 copy-start.2
Sparse Core Ops, SparseCore 0:
  40.7 204.3 all-reduce.2
where the time goes:
time: 279 us; the launch traced here: 278 us
  waiting for transfers between devices  221 us (79%)
  blocking collectives  18.1 us (6%)
  between operations  13.6 us (5%)
  starting transfers between devices  12.9 us (5%)
  local copies, waits for them, and re-layouts  5.79 us (2%)
  matrix products  5.18 us (2%)
    psum x1, waiting for transfers between devices, broadcast(): return lax.psum(jnp.where(mine, array, jnp.zeros_like(array)), axis)  207 us
    all_to_all x1, blocking collectives, shards(): lax.all_to_all(attended, 'hd', split_axis=0, concat_axis=1, tiled=True)  18.1 us
    all_to_all x1, waiting for transfers between devices, shards(): lax.all_to_all(values, 'hd', split_axis=1, concat_axis=0, tiled=True)  8 us
    all_to_all x1, starting transfers between devices, shards(): lax.all_to_all(keys, 'hd', split_axis=1, concat_axis=0, tiled=True)  6.03 us
    all_to_all x1, waiting for transfers between devices, shards(): lax.all_to_all(keys, 'hd', split_axis=1, concat_axis=0, tiled=True)  5.68 us
  transfers between devices with their start and end apart: 4, of which 3 were waited for; matrix products, arithmetic and copies ran while one was open for 1% of the time, Pallas kernels for 0%

commit v1 on v0

--- a/solution.py
+++ b/solution.py
@@ -11,7 +11,7 @@
 
 def broadcast(array, axis, root):
     mine = lax.axis_index(axis) == root
-    return lax.psum(jnp.where(mine, array, jnp.zeros_like(array)), axis)
+    return jnp.sum(lax.all_gather(jnp.where(mine, array, jnp.zeros_like(array)), axis), axis=0)
 
 
 def head_attention(query_part, key_part, value_part, visible, scaling):

time: 279 us -> 198 us (0.71)
  waiting for transfers between devices: 221 us -> 129 us
  other arithmetic: 1.73 us -> 6.66 us
  matrix products: 5.18 us -> 9.43 us
    psum x1 -> x0, waiting for transfers between devices: 207 us -> none  [broadcast(): return lax.psum(jnp.where(mine, array, jnp.zeros_like(array)), axis)]
    all_gather x0 -> x2, waiting for transfers between devices: none -> 114 us  [broadcast(): lax.all_gather(jnp.where(mine, array, jnp.zeros_like(array)), axis)]
    reduce_sum x0 -> x2, other arithmetic: none -> 3.76 us  [broadcast(): jnp.sum(lax.all_gather(jnp.where(mine, array, jnp.zeros_like(array)), axi...]
  transfers between devices with their start and end apart: 4 -> 5, of which waited for: 3 -> 4; matrix products, arithmetic and copies ran while one was open for 1% -> 6% of each run, Pallas kernels for 0% -> 0%
where the time goes in v1:
time: 198 us; the launch traced here: 195 us
  waiting for transfers between devices  129 us (65%)
  blocking collectives  17.5 us (9%)
  between operations  13.7 us (7%)
  starting transfers between devices  13 us (7%)
  matrix products  9.43 us (5%)
  other arithmetic  6.66 us (3%)
  local copies, waits for them, and re-layouts  5.09 us (3%)
    all_gather x2, waiting for transfers between devices, broadcast(): lax.all_gather(jnp.where(mine, array, jnp.zeros_like(array)), axis)  114 us
    all_to_all x1, blocking collectives, shards(): lax.all_to_all(attended, 'hd', split_axis=0, concat_axis=1, tiled=True)  17.5 us
    all_to_all x1, waiting for transfers between devices, shards(): lax.all_to_all(values, 'hd', split_axis=1, concat_axis=0, tiled=True)  7.97 us
    all_to_all x1, waiting for transfers between devices, shards(): lax.all_to_all(keys, 'hd', split_axis=1, concat_axis=0, tiled=True)  6.5 us
    all_to_all x1, starting transfers between devices, shards(): lax.all_to_all(keys, 'hd', split_axis=1, concat_axis=0, tiled=True)  6.03 us
    dot_general x8, matrix products, head_attention(): jnp.einsum('qd,kd->qk', query_part, key_part, preferred_element_type=jnp....  5.37 us
    dot_general x8, matrix products, head_attention(): mixture = jnp.dot(weights, value_part, preferred_element_type=jnp.float32)  4.06 us
  transfers between devices with their start and end apart: 5, of which 4 were waited for; matrix products, arithmetic and copies ran while one was open for 6% of the time, Pallas kernels for 0%

profile of v1, /device:TPU:98, one launch (start us, length us, event | category | flops | bytes accessed | tf_op | source)
XLA Modules:
  0.0 194.7 jit_solution(13702795959234804953)
XLA Ops:
  6.5 0.9 copy-done
  8.1 6.0 %all-to-all-start = ((bf16[64,8,128]{2,0,1:T(8,128)(2,1)}), bf16[64,8,128]{2,0,1:T(8,128)(2,1)S(1)}, u32[]{:S(2)}, u32[]{:S(2)}) async-start(bf16[64,8,128]{2,0,1:T(8,128)(2,1)} %copy_bitcast_fusion.2), calls=%async_computation | async-start | bytes 262144 | tf_op jit(solution)/shard_map/all_to_all | solution.py:34
  14.1 1.6 copy_bitcast_fusion.1
  15.7 6.5 %all-to-all-done = bf16[64,8,128]{2,0,1:T(8,128)(2,1)S(1)} async-done(((bf16[64,8,128]{2,0,1:T(8,128)(2,1)}), bf16[64,8,128]{2,0,1:T(8,128)(2,1)S(1)}, u32[]{:S(2)}, u32[]{:S(2)}) %all-to-all-start) | async-done | bytes 131104 | tf_op jit(solution)/shard_map/all_to_all | solution.py:34
  22.2 3.4 %all-to-all-start.2 = ((bf16[64,8,128]{2,0,1:T(8,128)(2,1)}), bf16[64,8,128]{2,0,1:T(8,128)(2,1)S(1)}, u32[]{:S(2)}, u32[]{:S(2)}) async-start(bf16[64,8,128]{2,0,1:T(8,128)(2,1)} %copy_bitcast_fusion.1), calls=%async_computation.2 | async-start | bytes 262144 | tf_op jit(solution)/shard_map/all_to_all | solution.py:35
  25.7 8.0 %all-to-all-done.2 = bf16[64,8,128]{2,0,1:T(8,128)(2,1)S(1)} async-done(((bf16[64,8,128]{2,0,1:T(8,128)(2,1)}), bf16[64,8,128]{2,0,1:T(8,128)(2,1)S(1)}, u32[]{:S(2)}, u32[]{:S(2)}) %all-to-all-start.2) | async-done | bytes 131104 | tf_op jit(solution)/shard_map/all_to_all | solution.py:35
  33.6 0.7 fusion.66
  34.4 0.7 all-gather.5.cloned.1.call-update
  35.1 0.8 copy.27
  35.9 3.5 %all-to-all-start.1 = ((bf16[64,8,512]{2,0,1:T(8,128)(2,1)}), bf16[64,8,512]{2,0,1:T(8,128)(2,1)S(1)}, u32[]{:S(2)}, u32[]{:S(2)}) async-start(bf16[64,8,512]{2,0,1:T(8,128)(2,1)} %bitcast.60), calls=%async_computation.1 | async-start | bytes 1048576 | tf_op jit(solution)/shard_map/all_to_all | solution.py:33
  39.5 56.7 %all-gather.3.cloned.1.call-done = bf16[32,256,128]{2,1,0:T(8,128)(2,1)} async-done(((bf16[1,256,128]{2,1,0:T(8,128)(2,1)}), bf16[32,256,128]{2,1,0:T(8,128)(2,1)}) %all-gather.3.cloned.1.call-update) | async-done | bytes 2097168 | tf_op jit(solution)/shard_map/all_gather | solution.py:14
  96.2 1.9 reduce_sum.96
  98.4 0.7 fusion.40
  99.4 0.7 fusion.38
  100.1 1.6 fusion.70
  101.7 0.9 fusion.71
  102.6 0.9 fusion.72
  104.0 0.9 fusion.75
  105.0 57.5 %all-gather.5.cloned.1.call-done = bf16[32,256,128]{2,1,0:T(8,128)(2,1)} async-done(((bf16[1,256,128]{2,1,0:T(8,128)(2,1)}), bf16[32,256,128]{2,1,0:T(8,128)(2,1)}) %all-gather.5.cloned.1.call-update) | async-done | bytes 2097168 | tf_op jit(solution)/shard_map/all_gather | solution.py:14
  162.5 1.9 reduce_sum.97
  164.4 1.3 fusion.23
  165.7 1.3 fusion.22
  169.6 17.5 %all_to_all.70 = bf16[8,64,512]{2,1,0:T(8,128)(2,1)S(1)} all-to-all(bf16[8,64,512]{2,1,0:T(8,128)(2,1)S(1)} %bitcast.61), channel_id=1, replica_groups=mesh['blk'=32,'hd'=8] {'hd'}, dimensions={0} | all-to-all | bytes 1048576 | tf_op jit(solution)/shard_map/all_to_all | solution.py:69
  187.1 0.8 copy.23
  (50 shorter events, 4.4 us)
Async XLA Ops:
  6.5 0.9 copy-start
  7.4 27.6 %copy-start.1 = (bf16[64,4096]{1,0:T(8,128)(2,1)S(1)}, bf16[64,4096]{1,0:T(8,128)(2,1)}, u32[]{:S(2)}) copy-start(bf16[64,4096]{1,0:T(8,128)(2,1)} %param.3) | copy-start | bytes 1572868
  8.1 14.1 %all-to-all-start = ((bf16[64,8,128]{2,0,1:T(8,128)(2,1)}), bf16[64,8,128]{2,0,1:T(8,128)(2,1)S(1)}, u32[]{:S(2)}, u32[]{:S(2)}) async-start(bf16[64,8,128]{2,0,1:T(8,128)(2,1)} %copy_bitcast_fusion.2), calls=%async_computation | async-start | bytes 262144 | tf_op jit(solution)/shard_map/all_to_all | solution.py:34
  22.2 11.4 %all-to-all-start.2 = ((bf16[64,8,128]{2,0,1:T(8,128)(2,1)}), bf16[64,8,128]{2,0,1:T(8,128)(2,1)S(1)}, u32[]{:S(2)}, u32[]{:S(2)}) async-start(bf16[64,8,128]{2,0,1:T(8,128)(2,1)} %copy_bitcast_fusion.1), calls=%async_computation.2 | async-start | bytes 262144 | tf_op jit(solution)/shard_map/all_to_all | solution.py:35
  25.6 70.6 %all-gather.3.cloned.1.call-start = ((), (), s32[]{:S(2)}) async-start(), calls=%async_computation.4 | async-start | bytes 2162688 | tf_op jit(solution)/shard_map/all_gather | solution.py:14
  34.3 128.2 %all-gather.5.cloned.1.call-start = ((), (), s32[]{:S(2)}) async-start(), calls=%async_computation.5 | async-start | bytes 2162688 | tf_op jit(solution)/shard_map/all_gather | solution.py:14
  35.9 62.1 %all-to-all-start.1 = ((bf16[64,8,512]{2,0,1:T(8,128)(2,1)}), bf16[64,8,512]{2,0,1:T(8,128)(2,1)S(1)}, u32[]{:S(2)}, u32[]{:S(2)}) async-start(bf16[64,8,512]{2,0,1:T(8,128)(2,1)} %bitcast.60), calls=%async_computation.1 | async-start | bytes 1048576 | tf_op jit(solution)/shard_map/all_to_all | solution.py:33
  39.4 64.3 %copy-start.12 = (pred[512]{0:T(512)(128)(4,1)}, pred[512]{0:T(512)(128)(4,1)S(1)}, u32[]{:S(2)}) copy-start(pred[512]{0:T(512)(128)(4,1)S(1)} %iota_compare_fusion.1) | copy-start | bytes 1540
  98.3 4.2 %copy-start.2 = (f32[256,512]{0,1:T(8,128)}, f32[256,512]{0,1:T(8,128)S(1)}, u32[]{:S(2)}) copy-start(f32[256,512]{0,1:T(8,128)S(1)} %get-tuple-element.12) | copy-start | bytes 1572868
  98.3 4.2 %copy-start.7 = (f32[256]{0:T(256)}, f32[256]{0:T(256)S(1)}, u32[]{:S(2)}) copy-start(f32[256]{0:T(256)S(1)} %get-tuple-element.11) | copy-start | bytes 3076
  99.3 4.1 %copy-start.9 = (f32[256]{0:T(256)}, f32[256]{0:T(256)S(1)}, u32[]{:S(2)}) copy-start(f32[256]{0:T(256)S(1)} %get-tuple-element.13) | copy-start | bytes 3076
  99.3 4.4 %copy-start.4 = (f32[256,512]{0,1:T(8,128)}, f32[256,512]{0,1:T(8,128)S(1)}, u32[]{:S(2)}) copy-start(f32[256,512]{0,1:T(8,128)S(1)} %get-tuple-element.14) | copy-start | bytes 1572868
  104.9 60.8 %copy-start.10 = (f32[256]{0:T(256)S(1)}, f32[256]{0:T(256)}, u32[]{:S(2)}) copy-start(f32[256]{0:T(256)} %copy-done.9) | copy-start | bytes 3076
  104.9 60.8 %copy-start.11 = (f32[256]{0:T(256)S(1)}, f32[256]{0:T(256)}, u32[]{:S(2)}) copy-start(f32[256]{0:T(256)} %fusion.38) | copy-start | bytes 3076
  105.0 62.1 %copy-start.3 = (f32[256,512]{0,1:T(8,128)S(1)}, f32[256,512]{0,1:T(8,128)}, u32[]{:S(2)}) copy-start(f32[256,512]{0,1:T(8,128)} %get-tuple-element.16) | copy-start | bytes 1572868
  105.0 62.1 %copy-start.8 = (f32[256]{0:T(256)S(1)}, f32[256]{0:T(256)}, u32[]{:S(2)}) copy-start(f32[256]{0:T(256)} %get-tuple-element.15) | copy-start | bytes 3076
  164.4 3.0 %copy-start.6 = (f32[256]{0:T(256)S(1)}, f32[256]{0:T(256)}, u32[]{:S(2)}) copy-start(f32[256]{0:T(256)} %get-tuple-element.17) | copy-start | bytes 3076
  165.7 2.1 %copy-start.5 = (f32[256]{0:T(256)S(1)}, f32[256]{0:T(256)}, u32[]{:S(2)}) copy-start(f32[256]{0:T(256)} %get-tuple-element.19) | copy-start | bytes 3076
Sparse Core Ops, SparseCore 0:
  34.4 61.6 all-gather.2
  98.0 64.4 all-gather.4
